TPU v7x, 128 devices: a whole 4x4x4 slice. The times are simulated.
128 devices in a mesh: wide: 16 (over y, z), grp: 8 (over x, core).
Axes of the slice: x: 4, y: 4, z: 4, core: 2. Of those that a mesh axis runs over, the one named last changes fastest.
Arguments:
- eta_hat: bfloat16 [2, 2048, 2048], P(None, ('wide', 'grp')), may hold values from -0.0008544922 to 0.0008544922
- phi_hat: bfloat16 [2, 2048, 2048], P(None, ('wide', 'grp')), may hold values from -0.00061035156 to 0.00061035156
- patch_tiles: int32 [256], replicated, may hold values from 0 to 1023, as said below
- fraction: bfloat16 [2, 128, 64, 128, 128], P(None, ('wide', 'grp')), may hold values from 0 to 1
Outputs:
- surface: float32 [2048, 2048], P(('wide', 'grp'))
- fraction_next: bfloat16 [2, 128, 64, 128, 128], P(None, ('wide', 'grp'))
- tendency: float32 [2, 2048, 2048], P(None, ('wide', 'grp'))
Inputs may be any that keep to these rules, and one draw needn't show every extreme that they name: `patch_tiles`: for each g below 8, entries g * 32 to (g + 1) * 32 - 1 are distinct tiles, in ascending order, whose column t % 32 lies in [g * 4, (g + 1) * 4). Of these, the tiles of one band (rows (t // 32) // 2 equal) are at most 8, and in every group one band holds exactly 8.
All inputs are finite; a program needn't handle non-finite values.
Results may differ from a plain program's by a relative error of at most 0.019.
Values may be sent and summed in bfloat16 or wider, within the bound.
A program may use at most 192 MiB of HBM per device.

v0:
```python
import math
import jax
import jax.numpy as jnp
from jax import lax
from jax.sharding import PartitionSpec as P

RADIX = 32
TS = 64
Z_BOTTOM = -2.0
Z_TOP = 2.0
DECAY_RATE = 0.5
COURANT = 0.3


def for_sending(shard):

    def short(part):
        return part.astype(jnp.bfloat16) if part.dtype == jnp.float32 else part

    return jax.tree.map(short, shard)


def refine(field):
    return jnp.repeat(jnp.repeat(field, 2, axis=0), 2, axis=1)


def upwind_flux(values, speeds, axis):
    widths = tuple(((1, 1) if dim_index == axis else (0, 0) for dim_index in range(3)))
    padded = jnp.pad(values, widths, mode="edge")
    speed_pad = jnp.pad(speeds, widths, mode="edge")
    count_faces = padded.shape[axis] - 1
    left_vals = lax.slice_in_dim(padded, 0, count_faces, axis=axis)
    right_vals = lax.slice_in_dim(padded, 1, count_faces + 1, axis=axis)
    face_speed = 0.5 * (
        lax.slice_in_dim(speed_pad, 0, count_faces, axis=axis)
        + lax.slice_in_dim(speed_pad, 1, count_faces + 1, axis=axis)
    )
    face_flux = jnp.maximum(face_speed, 0.0) * left_vals + jnp.minimum(face_speed, 0.0) * right_vals
    return lax.slice_in_dim(face_flux, 1, count_faces, axis=axis) - lax.slice_in_dim(
        face_flux, 0, count_faces - 1, axis=axis
    )


def patch_step(state, height, along_x, along_y):
    levels = state.shape[0]
    side = state.shape[1]
    spacing = (Z_TOP - Z_BOTTOM) / levels
    level_z = (Z_BOTTOM + (jnp.arange(levels, dtype=jnp.float32) + 0.5) * spacing)[:, None, None]
    fine_h = refine(height)[None]
    from_sea = jnp.clip((fine_h - level_z) / spacing + 0.5, 0.0, 1.0)
    position = jnp.arange(side, dtype=jnp.float32)
    edge_dist = jnp.minimum(position, side - 1.0 - position)
    distance = jnp.minimum(edge_dist[:, None], edge_dist[None, :])
    weight = 0.3 + 0.7 * jnp.exp(-8.0 * distance / side)
    blended = weight * from_sea + (1.0 - weight) * state.astype(jnp.float32)
    profile = jnp.exp(DECAY_RATE * (level_z - Z_TOP))
    speed_x = refine(along_x)[None] * profile
    speed_y = refine(along_y)[None] * profile
    moved = blended - COURANT * (
        upwind_flux(blended, speed_x, 2) + upwind_flux(blended, speed_y, 1)
    )
    updated = jnp.clip(moved, 0.0, 1.0)
    column = Z_BOTTOM + spacing * jnp.sum(updated, axis=0)
    coarse = column.reshape(side // 2, 2, side // 2, 2).mean(axis=(1, 3))
    return (updated.astype(jnp.bfloat16), coarse)


def small_tables(length):
    index_row = jnp.arange(length, dtype=jnp.int32)
    phase = index_row[:, None] * index_row[None, :] % length
    angle = phase.astype(jnp.float32) * (2.0 * math.pi / length)
    return (jnp.cos(angle).astype(jnp.bfloat16), jnp.sin(angle).astype(jnp.bfloat16))


def contract(data, table, pattern):
    return jnp.einsum(pattern, data, table, preferred_element_type=jnp.float32)


def factored_transform(real_in, imag_in, direction_sign, real_only):
    length = real_in.shape[-1]
    leading = real_in.shape[:-1]
    inner_size = length // RADIX
    cos_p, sin_p = small_tables(RADIX)
    cos_q, sin_q = small_tables(inner_size)
    split_re = real_in.reshape(leading + (RADIX, inner_size))
    segment_re = contract(split_re, cos_p, "...pq,pk->...kq")
    segment_im = direction_sign * contract(split_re, sin_p, "...pq,pk->...kq")
    if imag_in is not None:
        split_im = imag_in.reshape(leading + (RADIX, inner_size))
        segment_re = segment_re - direction_sign * contract(split_im, sin_p, "...pq,pk->...kq")
        segment_im = segment_im + contract(split_im, cos_p, "...pq,pk->...kq")
    first_idx = jnp.arange(RADIX, dtype=jnp.int32)[:, None]
    second_idx = jnp.arange(inner_size, dtype=jnp.int32)[None, :]
    angle = (first_idx * second_idx % length).astype(jnp.float32) * (2.0 * math.pi / length)
    twist_cos = jnp.cos(angle)
    twist_sin = jnp.sin(angle)
    turned_re = (segment_re * twist_cos - direction_sign * segment_im * twist_sin).astype(
        jnp.bfloat16
    )
    turned_im = (segment_im * twist_cos + direction_sign * segment_re * twist_sin).astype(
        jnp.bfloat16
    )
    out_re = contract(turned_re, cos_q, "...kq,qm->...km") - direction_sign * contract(
        turned_im, sin_q, "...kq,qm->...km"
    )
    out_re = jnp.swapaxes(out_re, -1, -2).reshape(leading + (length,))
    if real_only:
        return out_re
    out_im = contract(turned_im, cos_q, "...kq,qm->...km") + direction_sign * contract(
        turned_re, sin_q, "...kq,qm->...km"
    )
    out_im = jnp.swapaxes(out_im, -1, -2).reshape(leading + (length,))
    return (out_re, out_im)


def signed_waves(index_values, length):
    signed = (index_values + length // 2) % length - length // 2
    return signed.astype(jnp.float32) * (2.0 * math.pi / length)


def shards(eta_hat, phi_hat, patch_tiles, fraction):
    row_count = eta_hat.shape[1]
    length = eta_hat.shape[2]
    n_wide = lax.axis_size("wide")
    me_wide = lax.axis_index("wide")
    me_grp = lax.axis_index("grp")
    me_flat = lax.axis_index(("wide", "grp"))
    wave_cols = signed_waves(jnp.arange(length, dtype=jnp.int32), length)
    wave_rows = signed_waves(me_flat * row_count + jnp.arange(row_count, dtype=jnp.int32), length)
    phi_re = phi_hat[0].astype(jnp.float32)
    phi_im = phi_hat[1].astype(jnp.float32)
    real_in = jnp.stack(
        [
            eta_hat[0],
            (-wave_rows[:, None] * phi_im).astype(jnp.bfloat16),
            (-wave_cols[None, :] * phi_im).astype(jnp.bfloat16),
        ]
    )
    imag_in = jnp.stack(
        [
            eta_hat[1],
            (wave_rows[:, None] * phi_re).astype(jnp.bfloat16),
            (wave_cols[None, :] * phi_re).astype(jnp.bfloat16),
        ]
    )
    half_re, half_im = factored_transform(real_in, imag_in, 1.0, False)
    inverse_rows = jnp.swapaxes(
        jnp.concatenate([half_re.astype(jnp.bfloat16), half_im.astype(jnp.bfloat16)]), 1, 2
    )
    turned = lax.all_to_all(inverse_rows, ("wide", "grp"), split_axis=1, concat_axis=2, tiled=True)
    physical = factored_transform(turned[0:3], turned[3:6], 1.0, True)
    band_fields = lax.all_to_all(
        physical.astype(jnp.bfloat16), "grp", split_axis=2, concat_axis=1, tiled=True
    ).astype(physical.dtype)
    band_rows = band_fields.shape[1]
    band_cols = band_fields.shape[2]
    tile_rows = band_rows // TS
    tile_cols = band_cols // TS
    tiles_side = length // TS
    per_group = 2 * n_wide
    group_list = lax.dynamic_slice_in_dim(patch_tiles, me_grp * per_group, per_group)
    row_of = group_list // tiles_side
    col_of = group_list % tiles_side - me_grp * tile_cols
    my_ranks = jnp.arange(2, dtype=jnp.int32) * n_wide + me_wide
    local_t = jnp.arange(tile_rows * tile_cols, dtype=jnp.int32)
    tile_id = (
        (me_wide * tile_rows + local_t // tile_cols) * tiles_side
        + me_grp * tile_cols
        + local_t % tile_cols
    )
    matches = tile_id[:, None] == group_list[None, :]
    active = jnp.any(matches, axis=1)
    rank_index = jnp.sum(
        jnp.where(matches, jnp.arange(per_group, dtype=jnp.int32)[None, :], 0), axis=1
    )
    column_strip = lax.all_gather(
        band_fields.astype(jnp.bfloat16), "wide", axis=1, tiled=True
    ).astype(band_fields.dtype)

    def pick_strip(rank):
        return lax.dynamic_slice(
            column_strip, (0, row_of[rank] * TS, col_of[rank] * TS), (3, TS, TS)
        )

    footprints = jax.vmap(pick_strip)(my_ranks)
    new_states, coarse = jax.vmap(patch_step)(
        fraction[:, 0], footprints[:, 0], footprints[:, 1], footprints[:, 2]
    )
    coarse_flat = coarse.reshape(2, TS * TS)
    every_result = (
        lax.all_gather(
            coarse_flat.reshape(2, 1, TS * TS).astype(jnp.bfloat16), "wide", axis=1, tiled=True
        )
        .astype(jnp.float32)
        .reshape(per_group, TS * TS)
    )
    picked = every_result[rank_index]
    band_tiles = (
        band_fields[0]
        .reshape(tile_rows, TS, tile_cols, TS)
        .transpose(0, 2, 1, 3)
        .reshape(tile_rows * tile_cols, TS * TS)
    )
    corrected = jnp.where(active[:, None], picked, band_tiles)
    surface_band = (
        corrected.reshape(tile_rows, tile_cols, TS, TS)
        .transpose(0, 2, 1, 3)
        .reshape(band_rows, band_cols)
    )
    surface = lax.all_to_all(
        for_sending(surface_band), "grp", split_axis=0, concat_axis=1, tiled=True
    ).astype(surface_band.dtype)
    along_x = physical[1]
    along_y = physical[2]
    drive = (-(surface + 0.5 * (along_x * along_x + along_y * along_y))).astype(jnp.bfloat16)
    drive_re, drive_im = factored_transform(drive, None, -1.0, False)
    pair_rows = jnp.swapaxes(
        jnp.stack([drive_re.astype(jnp.bfloat16), drive_im.astype(jnp.bfloat16)]), 1, 2
    )
    pair_cols = lax.all_to_all(pair_rows, ("wide", "grp"), split_axis=1, concat_axis=2, tiled=True)
    spec_re, spec_im = factored_transform(pair_cols[0], pair_cols[1], -1.0, False)
    tendency = jnp.stack([spec_re, spec_im]) * (1.0 / length)
    return (surface, new_states[:, None], tendency)


def solution(mesh):
    placed = (
        P(None, ("wide", "grp"), None),
        P(None, ("wide", "grp"), None),
        P(),
        P(None, ("wide", "grp"), None, None, None),
    )
    return jax.shard_map(
        shards,
        mesh=mesh,
        in_specs=placed,
        out_specs=(
            P(("wide", "grp"), None),
            P(None, ("wide", "grp"), None, None, None),
            P(None, ("wide", "grp"), None),
        ),
        check_vma=False,
    )
```

profile of v0, /device:TPU:1, one launch (start us, length us, event | category | flops | bytes accessed | tf_op | source)
XLA Modules:
  0.0 338.8 jit_solution(14497222716978649175)
XLA Ops:
  7.4 0.9 fusion.251
  8.4 1.0 fusion.42
  13.8 0.8 convert_element_type.411
  15.0 0.8 convert_element_type.408
  15.9 4.1 %copy.124 = bf16[6,2048,16]{2,0,1:T(8,128)(2,1)} copy(bf16[6,2048,16]{1,2,0:T(8,128)(2,1)S(1)} %maximum_bitcast_fusion) | data formatting | bytes 786432 | tf_op jit(solution)/shard_map/transpose | solution.py:147
  20.0 5.6 %reshape.527 = bf16[128,2,768]{2,1,0:T(2,128)(2,1)S(1)} reshape(bf16[2048,6,16]{2,1,0:T(8,128)(2,1)} %bitcast.240) | data formatting | bytes 786432
  25.6 24.1 %all_to_all.58 = bf16[128,2,768]{2,1,0:T(2,128)(2,1)S(1)} all-to-all(bf16[128,2,768]{2,1,0:T(2,128)(2,1)S(1)} %reshape.527), channel_id=1, replica_groups=mesh['wide'=16,'grp'=8] {'wide','grp'}, dimensions={0} | all-to-all | bytes 786432 | tf_op jit(solution)/shard_map/all_to_all | solution.py:150
  49.7 4.8 %reshape.528 = bf16[2048,6,16]{2,1,0:T(8,128)(2,1)} reshape(bf16[128,2,768]{2,1,0:T(2,128)(2,1)S(1)} %all_to_all.58) | data formatting | bytes 786432
  54.6 6.1 %copy.158 = bf16[6,128,16,16]{2,1,3,0:T(8,128)(2,1)S(1)} copy(bf16[6,128,16,16]{3,0,2,1:T(8,128)(2,1)} %bitcast.239) | data formatting | bytes 786432 | tf_op jit(solution)/shard_map/all_to_all | solution.py:150
  60.7 1.9 fusion.249
  62.6 4.3 %copy.126 = bf16[3,16,128,16]{3,2,1,0:T(8,128)(2,1)S(1)} copy(bf16[3,16,128,16]{1,2,3,0:T(8,128)(2,1)} %get-tuple-element.58) | data formatting | bytes 393216 | tf_op jit(solution)/shard_map/slice | solution.py:151
  67.7 1.2 fusion.99
  69.0 1.3 fusion.106
  70.2 3.1 copy.127
  74.2 1.5 convolution_add_fusion
  75.6 1.5 convolution_subtract_fusion.1
  77.9 3.4 %copy.159 = bf16[3,16,64,32]{1,0,3,2:T(4,128)(2,1)S(1)} copy(bf16[3,16,64,32]{2,3,1,0:T(8,128)(2,1)S(1)} %get-tuple-element.82) | data formatting | bytes 393216 | tf_op jit(solution)/shard_map/convert_element_type | solution.py:153
  81.3 1.9 reshape.529
  83.2 9.3 %all_to_all.59 = bf16[8,2,6144]{2,1,0:T(2,128)(2,1)S(1)} all-to-all(bf16[8,2,6144]{2,1,0:T(2,128)(2,1)S(1)} %reshape.529), channel_id=1, replica_groups=mesh['wide'=16,'grp'=8] {'grp'}, dimensions={0} | all-to-all | bytes 393216 | tf_op jit(solution)/shard_map/all_to_all | solution.py:152
  92.5 2.0 reshape.530
  94.5 2.0 copy.161
  99.9 1.0 copy.160
  101.1 39.6 %all-gather.2.cloned.1.call-done = bf16[3,2048,256]{2,1,0:T(8,128)(2,1)} async-done(((bf16[3,128,256]{2,1,0:T(8,128)(2,1)}), bf16[3,2048,256]{2,1,0:T(8,128)(2,1)}) %all-gather.2.cloned.1.call-update) | async-done | bytes 3145744 | tf_op jit(solution)/shard_map/all_gather | solution.py:176
  140.7 5.1 %convert_element_type.418 = f32[3,2048,256]{2,1,0:T(8,128)} convert(bf16[3,2048,256]{2,1,0:T(8,128)(2,1)} %all-gather.2.cloned.1.call-done) | non-fusion elementwise | flops 1572864 | bytes 9437184 | tf_op jit(solution)/shard_map/convert_element_type | solution.py:178
  145.8 5.9 %while.1 = (s32[]{:T(128)}, f32[3,2048,256]{2,1,0:T(8,128)}, s32[2,3]{1,0:T(2,128)S(1)}, f32[2,3,64,64]{3,2,1,0:T(8,128)S(1)}, s32[]{:T(128)}) while((s32[]{:T(128)}, f32[3,2048,256]{2,1,0:T(8,128)}, s32[2,3]{1,0:T(2,128)S(1)}, f32[2,3,64,64]{3,2,1,0:T(8,128)S(1)}, s32[]{:T(128)}) %tuple.55), condition=%wide.while_cond, body=%wide.while_body.sunk | while | flops 2 | bytes 147581 | solution.py:181
  146.4 2.3 bitcast_dynamic-update-slice_fusion.2
  149.3 2.3 bitcast_dynamic-update-slice_fusion.2
  152.3 0.9 slice_bitcast_fusion.1
  153.6 3.9 %fusion.8 = f32[2,64,128,128]{3,2,1,0:T(8,128)S(1)} fusion(bf16[2,1,64,128,128]{4,3,2,1,0:T(8,128)(2,1)} %param.7, f32[128,128]{1,0:T(8,128)S(1)} %get-tuple-element.81, f32[64]{0:T(128)S(1)} %fusion.129, f32[2,128,128]{2,1,0:T(8,128)S(1)} %copy.134, f32[128,128]{1,0:T(8,128)S(1)} %get-tuple-element.80), kind=kLoop, calls=%fused_computation.22 | loop fusion | flops 16777216 | bytes 12845312 | tf_op jit(solution)/shard_map/vmap()/add | solution.py:55
  157.6 7.7 %fusion.246 = (f32[2,64,128,1]{3,2,1,0:T(8,128)}, f32[2,64,128,1]{3,2,1,0:T(8,128)}) fusion(f32[2,64,128,128]{3,2,1,0:T(8,128)S(1)} %fusion.8), kind=kLoop, calls=%fused_computation.353 | loop fusion | bytes 262144 | tf_op jit(solution)/shard_map/vmap(jit(_pad))/slice | solution.py:29
  166.5 5.4 %broadcast_multiply_fusion.1 = (f32[2,64,128,128]{3,2,1,0:T(8,128)}, f32[2,64,128,128]{3,2,1,0:T(8,128)S(1)}) fusion(f32[64]{0:T(128)S(1)} %multiply_exponential_fusion, f32[2,128,128]{2,1,0:T(8,128)S(1)} %copy.137, f32[2,128,128]{2,1,0:T(8,128)S(1)} %copy.139), kind=kLoop, calls=%fused_computation.25 | loop fusion | flops 4194304 | bytes 17039616 | tf_op jit(solution)/shard_map/vmap()/mul | solution.py:57
  171.9 3.2 copy-done.1
  175.2 13.3 %fusion.245 = (f32[2,64,128,1]{3,2,1,0:T(8,128)}, f32[2,64,128,1]{3,2,1,0:T(8,128)}) fusion(f32[2,64,128,128]{3,2,1,0:T(8,128)} %get-tuple-element.78), kind=kLoop, calls=%fused_computation.352 | loop fusion | bytes 262144 | tf_op jit(solution)/shard_map/vmap(jit(_pad))/slice | solution.py:30
  188.5 12.6 %fusion.3 = f32[2,64,129,128]{3,2,1,0:T(8,128)} fusion(f32[2,64,128,128]{3,2,1,0:T(8,128)S(1)} %bitcast.236, f32[2,64,1,128]{3,2,1,0:T(1,128)S(1)} %get-tuple-element.56, f32[2,64,1,128]{3,2,1,0:T(1,128)S(1)} %get-tuple-element.55, f32[2,64,1,128]{3,2,1,0:T(1,128)S(1)} %get-tuple-element.54, f32[2,64,128,128]{3,2,1,0:T(8,128)} %copy-done.1, ...), kind=kLoop, calls=%fused_computation.13 | loop fusion | flops 23248896 | bytes 25493504 | tf_op jit(solution)/shard_map/vmap()/add | solution.py:38
  201.1 25.7 %fusion.1 = f32[2,64,128,129]{3,2,1,0:T(8,128)} fusion(f32[2,64,128,128]{3,2,1,0:T(8,128)S(1)} %bitcast.236, f32[2,64,128,1]{3,2,1,0:T(8,128)} %get-tuple-element.52, f32[2,64,128,1]{3,2,1,0:T(8,128)} %get-tuple-element.51, f32[2,64,128,1]{3,2,1,0:T(8,128)} %get-tuple-element.50, f32[2,64,128,128]{3,2,1,0:T(8,128)} %get-tuple-element.78, ...), kind=kLoop, calls=%fused_computation.8 | loop fusion | flops 23248896 | bytes 25493504 | tf_op jit(solution)/shard_map/vmap()/add | solution.py:38
  226.8 22.0 %convert_bitcast_fusion = (bf16[2,1,64,128,128]{4,3,2,1,0:T(8,128)(2,1)}, f32[2,64,128,128]{3,2,1,0:T(8,128)}) fusion(f32[2,64,129,128]{3,2,1,0:T(8,128)} %fusion.3, f32[2,64,128,129]{3,2,1,0:T(8,128)} %fusion.1, bf16[2,1,64,128,128]{4,3,2,1,0:T(8,128)(2,1)} %param.7, f32[128,128]{1,0:T(8,128)S(1)} %get-tuple-element.81, f32[64]{0:T(128)S(1)} %fusion.129, ...), kind=kLoop, calls=%fused_computation.23 | loop fusion | flops 31457280 | bytes 50594048 | tf_op jit(solution)/shard_map/broadcast_in_dim | solution.py:223
  248.9 3.8 %reduce_sum.29 = f32[2,128,128]{2,1,0:T(8,128)S(1)} reduce(f32[2,64,128,128]{3,2,1,0:T(8,128)} %get-tuple-element.44, f32[]{:T(128)} %constant.200.clone.1), dimensions={1}, to_apply=%region_1.2 | reduce | flops 2064384 | bytes 8519684 | tf_op jit(solution)/shard_map/vmap()/reduce_sum | solution.py:63
  252.7 9.8 %add.508 = f32[2,64,2,64,2]{4,3,2,1,0:T(8,128)} reshape(f32[2,128,128]{2,1,0:T(8,128)S(1)} %multiply_add_fusion) | data formatting | bytes 262144 | tf_op jit(solution)/shard_map/vmap()/add | solution.py:63
  262.5 4.5 %reduce_sum.30 = f32[2,64,64]{2,1,0:T(8,128)S(1)} reduce(f32[2,64,2,64,2]{4,3,2,1,0:T(8,128)} %add.508, f32[]{:T(128)} %constant.200.clone.1), dimensions={2,4}, to_apply=%region_2.3 | reduce | flops 24576 | bytes 163844 | tf_op jit(solution)/shard_map/vmap()/reduce_sum | solution.py:64
  267.2 17.1 %all_gather.7 = bf16[2,16,4096]{2,0,1:T(2,128)(2,1)S(1)} all-gather(bf16[2,1,4096]{2,0,1:T(2,128)(2,1)S(1)} %convert_element_type.422), channel_id=1, replica_groups=mesh['wide'=16,'grp'=8] {'wide'}, dimensions={1}, use_global_device_ids=true | all-gather | bytes 278528 | tf_op jit(solution)/shard_map/all_gather | solution.py:191
  286.1 11.0 %all-to-all-start.2 = ((bf16[8,16,256]{2,1,0:T(8,128)(2,1)}), bf16[8,16,256]{2,1,0:T(8,128)(2,1)S(1)}, u32[]{:S(2)}, u32[]{:S(2)}) async-start(bf16[8,16,256]{2,1,0:T(8,128)(2,1)} %convert_element_type.425), calls=%async_computation.2 | async-start | bytes 131072 | tf_op jit(solution)/shard_map/all_to_all | solution.py:210
  297.5 4.4 %all-to-all-done.2 = bf16[8,16,256]{2,1,0:T(8,128)(2,1)S(1)} async-done(((bf16[8,16,256]{2,1,0:T(8,128)(2,1)}), bf16[8,16,256]{2,1,0:T(8,128)(2,1)S(1)}, u32[]{:S(2)}, u32[]{:S(2)}) %all-to-all-start.2) | async-done | bytes 65568 | tf_op jit(solution)/shard_map/all_to_all | solution.py:210
  305.6 1.5 reshape.531
  307.2 4.9 %all-to-all-start.3 = ((bf16[128,2,256]{2,1,0:T(2,128)(2,1)}), bf16[128,2,256]{2,1,0:T(2,128)(2,1)S(1)}, u32[]{:S(2)}, u32[]{:S(2)}) async-start(bf16[128,2,256]{2,1,0:T(2,128)(2,1)} %reshape.531), calls=%async_computation.3 | async-start | bytes 262144 | tf_op jit(solution)/shard_map/all_to_all | solution.py:220
  312.8 9.3 %all-to-all-done.3 = bf16[128,2,256]{2,1,0:T(2,128)(2,1)S(1)} async-done(((bf16[128,2,256]{2,1,0:T(2,128)(2,1)}), bf16[128,2,256]{2,1,0:T(2,128)(2,1)S(1)}, u32[]{:S(2)}, u32[]{:S(2)}) %all-to-all-start.3) | async-done | bytes 131104 | tf_op jit(solution)/shard_map/all_to_all | solution.py:220
  322.7 2.0 copy.162
  324.9 1.1 copy.150
  326.8 1.1 copy.151
  (142 shorter events, 26.0 us)
Async XLA Ops:
  7.2 133.5 %all-gather.2.cloned.1.call-start = ((), (), s32[]{:S(2)}) async-start(), calls=%async_computation.4 | async-start | bytes 3342336 | tf_op jit(solution)/shard_map/all_gather | solution.py:176
  7.3 6.5 %copy-start.3 = (f32[32,64]{1,0:T(8,128)}, f32[32,64]{1,0:T(8,128)S(1)}, u32[]{:S(2)}) copy-start(f32[32,64]{1,0:T(8,128)S(1)} %get-tuple-element.88) | copy-start | bytes 24580
  62.6 7.6 %copy-start.2 = (bf16[3,16,128,16]{1,2,3,0:T(8,128)(2,1)S(1)}, bf16[3,16,128,16]{1,2,3,0:T(8,128)(2,1)}, u32[]{:S(2)}) copy-start(bf16[3,16,128,16]{1,2,3,0:T(8,128)(2,1)} %get-tuple-element.57) | copy-start | bytes 589828
  70.2 6.9 %copy-start.4 = (f32[32,64]{1,0:T(8,128)S(1)}, f32[32,64]{1,0:T(8,128)}, u32[]{:S(2)}) copy-start(f32[32,64]{1,0:T(8,128)} %copy-done.3) | copy-start | bytes 24580
  77.1 19.5 %copy-start.8 = (s32[256]{0:T(256)S(1)}, s32[256]{0:T(256)}, u32[]{:S(2)}) copy-start(s32[256]{0:T(256)} %param.6) | copy-start | bytes 3076
  151.7 0.7 copy-start.5
  157.5 8.4 %copy-start = (f32[2,64,128,128]{3,2,1,0:T(8,128)}, f32[2,64,128,128]{3,2,1,0:T(8,128)S(1)}, u32[]{:S(2)}) copy-start(f32[2,64,128,128]{3,2,1,0:T(8,128)S(1)} %fusion.8) | copy-start | bytes 25165828
  166.4 22.1 %slice-start = ((s8[8388608]{0:T(1024)(128)(4,1)}), s8[4194304]{0:T(1024)(128)(4,1)S(1)}, s32[]{:S(2)}) async-start(s8[8388608]{0:T(1024)(128)(4,1)} %bitcast.235), calls=%async_computation.5 | async-start | bytes 8388608
  171.9 3.2 copy-start.1
  175.2 13.3 %slice-start.1 = ((s8[8388608]{0:T(1024)(128)(4,1)}), s8[4194304]{0:T(1024)(128)(4,1)S(1)}, s32[]{:S(2)}) async-start(s8[8388608]{0:T(1024)(128)(4,1)} %bitcast.235), calls=%async_computation.6 | async-start | bytes 8388608
  252.7 32.5 %copy-start.7 = (pred[2,4]{1,0:T(4,128)(4,1)S(1)}, pred[2,4]{1,0:T(4,128)(4,1)}, u32[]{:S(2)}) copy-start(pred[2,4]{1,0:T(4,128)(4,1)} %broadcast_in_dim.29) | copy-start | bytes 28
  262.5 39.9 %copy-start.6 = (f32[32,64]{1,0:T(8,128)S(1)}, f32[32,64]{1,0:T(8,128)}, u32[]{:S(2)}) copy-start(f32[32,64]{1,0:T(8,128)} %get-tuple-element.93) | copy-start | bytes 24580
  286.1 15.8 %all-to-all-start.2 = ((bf16[8,16,256]{2,1,0:T(8,128)(2,1)}), bf16[8,16,256]{2,1,0:T(8,128)(2,1)S(1)}, u32[]{:S(2)}, u32[]{:S(2)}) async-start(bf16[8,16,256]{2,1,0:T(8,128)(2,1)} %convert_element_type.425), calls=%async_computation.2 | async-start | bytes 131072 | tf_op jit(solution)/shard_map/all_to_all | solution.py:210
  307.2 14.9 %all-to-all-start.3 = ((bf16[128,2,256]{2,1,0:T(2,128)(2,1)}), bf16[128,2,256]{2,1,0:T(2,128)(2,1)S(1)}, u32[]{:S(2)}, u32[]{:S(2)}) async-start(bf16[128,2,256]{2,1,0:T(2,128)(2,1)} %reshape.531), calls=%async_computation.3 | async-start | bytes 262144 | tf_op jit(solution)/shard_map/all_to_all | solution.py:220
Sparse Core Ops, SparseCore 0:
  96.7 44.0 all-gather.1
where the time goes:
time: 346 us; the launch traced here: 339 us
  local copies, waits for them, and re-layouts  104 us (30%)
  other arithmetic  86.5 us (25%)
  waiting for transfers between devices  53.3 us (15%)
  blocking collectives  50.5 us (15%)
  starting transfers between devices  16 us (5%)
  between operations  15.4 us (4%)
  matrix products  13 us (4%)
    all_gather x1, waiting for transfers between devices, shards(): lax.all_gather(band_fields.astype(jnp.bfloat16), 'wide', axis=1, tiled=True)  39.6 us
    add x2, other arithmetic, upwind_flux(): jnp.maximum(face_speed, 0.0) * left_vals  38.3 us
    all_to_all x1, blocking collectives, shards(): lax.all_to_all(inverse_rows, ('wide', 'grp'), split_axis=1, concat_axis=2...  24.1 us
    broadcast_in_dim x1, other arithmetic, shards(): return (surface, new_states[:, None], tendency)  22 us
    unnamed x33, local copies, waits for them, and re-layouts  21.2 us
    all_gather x1, blocking collectives, shards(): lax.all_gather(coarse_flat.reshape(2, 1, TS * TS).astype(jnp.bfloat16), '...  17.1 us
    slice x2, local copies, waits for them, and re-layouts, upwind_flux(): speed_pad = jnp.pad(speeds, widths, mode='edge')  13.4 us
    dot_general x28, matrix products, contract(): return jnp.einsum(pattern, data, table, preferred_element_type=jnp.float32)  13 us
  transfers between devices with their start and end apart: 3, of which 3 were waited for; matrix products, arithmetic and copies ran while one was open for 2% of the time, Pallas kernels for 0%

commit v1 on v0

--- a/solution.py
+++ b/solution.py
@@ -10,6 +10,36 @@
 Z_TOP = 2.0
 DECAY_RATE = 0.5
 COURANT = 0.3
+
+
+def set_feed(xin, axis_k, x_local):
+    carry_out = xin.shape
+    shaped = xin.reshape(
+        *carry_out[:axis_k], x_local, carry_out[axis_k] // x_local, *carry_out[axis_k + 1 :]
+    )
+    return jnp.moveaxis(shaped, axis_k, 0)
+
+
+def waves_write(patch, dim_k):
+    f_now = list(patch.shape[1:])
+    f_now[dim_k] *= patch.shape[0]
+    return jnp.moveaxis(patch, 0, dim_k).reshape(f_now)
+
+
+def draw_the_spot(obj, bus_axis, local_values, my_tile):
+    w1 = lax.psum(1, axis_name=bus_axis)
+    lower = lax.axis_index(bus_axis)
+    reply, fresh = (w1, lower)
+    u1 = set_feed(obj, local_values, reply)
+    buffer = [u1[fresh]]
+    for num in range(1, reply):
+        current_value = u1[fresh ^ num]
+        res = lax.ppermute(
+            current_value, axis_name=bus_axis, perm=[(nth, nth ^ num) for nth in range(reply)]
+        )
+        buffer.append(res)
+    u1 = jnp.stack(buffer, axis=0)[fresh ^ jnp.arange(reply)]
+    return waves_write(u1, my_tile)
 
 
 def for_sending(shard):
@@ -207,9 +237,7 @@
         .transpose(0, 2, 1, 3)
         .reshape(band_rows, band_cols)
     )
-    surface = lax.all_to_all(
-        for_sending(surface_band), "grp", split_axis=0, concat_axis=1, tiled=True
-    ).astype(surface_band.dtype)
+    surface = draw_the_spot(for_sending(surface_band), "grp", 0, 1).astype(surface_band.dtype)
     along_x = physical[1]
     along_y = physical[2]
     drive = (-(surface + 0.5 * (along_x * along_x + along_y * along_y))).astype(jnp.bfloat16)

time: 346 us -> 350 us (1.012)
  starting transfers between devices: 16 us -> 20.7 us
    ppermute x0 -> x7, starting transfers between devices: none -> 14.2 us  [draw_the_spot(): lax.ppermute(current_value, axis_name=bus_axis, perm=[(nth, nth ^ num) fo...]
    all_to_all x1 -> x0, starting transfers between devices: 11 us -> none  [shards(): lax.all_to_all(for_sending(surface_band), 'grp', split_axis=0, concat_axi...]
    ppermute x0 -> x7, waiting for transfers between devices: none -> 4.76 us  [draw_the_spot(): lax.ppermute(current_value, axis_name=bus_axis, perm=[(nth, nth ^ num) fo...]
    all_to_all x1 -> x0, waiting for transfers between devices: 4.4 us -> none  [shards(): lax.all_to_all(for_sending(surface_band), 'grp', split_axis=0, concat_axi...]
    unnamed x33 -> x39, local copies, waits for them, and re-layouts: 21.2 us -> 21.2 us
  transfers between devices with their start and end apart: 3 -> 9, of which waited for: 3 -> 4; matrix products, arithmetic and copies ran while one was open for 2% -> 2% of each run, Pallas kernels for 0% -> 0%
where the time goes in v1:
time: 350 us; the launch traced here: 344 us
  local copies, waits for them, and re-layouts  104 us (30%)
  other arithmetic  87.3 us (25%)
  waiting for transfers between devices  53 us (15%)
  blocking collectives  50.2 us (14%)
  starting transfers between devices  20.7 us (6%)
  between operations  15.2 us (4%)
  matrix products  12.9 us (4%)
    all_gather x1, waiting for transfers between devices, shards(): lax.all_gather(band_fields.astype(jnp.bfloat16), 'wide', axis=1, tiled=True)  38.9 us
    add x2, other arithmetic, upwind_flux(): jnp.maximum(face_speed, 0.0) * left_vals  38.5 us
    all_to_all x1, blocking collectives, shards(): lax.all_to_all(inverse_rows, ('wide', 'grp'), split_axis=1, concat_axis=2...  23.8 us
    broadcast_in_dim x1, other arithmetic, shards(): return (surface, new_states[:, None], tendency)  22 us
    unnamed x39, local copies, waits for them, and re-layouts  21.2 us
    all_gather x1, blocking collectives, shards(): lax.all_gather(coarse_flat.reshape(2, 1, TS * TS).astype(jnp.bfloat16), '...  17.1 us
    ppermute x7, starting transfers between devices, draw_the_spot(): lax.ppermute(current_value, axis_name=bus_axis, perm=[(nth, nth ^ num) fo...  14.2 us
    slice x2, local copies, waits for them, and re-layouts, upwind_flux(): speed_pad = jnp.pad(speeds, widths, mode='edge')  13.4 us
  transfers between devices with their start and end apart: 9, of which 4 were waited for; matrix products, arithmetic and copies ran while one was open for 2% of the time, Pallas kernels for 0%

profile of v1, /device:TPU:1, one launch (start us, length us, event | category | flops | bytes accessed | tf_op | source)
XLA Modules:
  0.0 343.7 jit_solution(17321797187967450919)
XLA Ops:
  15.9 4.1 %copy.124 = bf16[6,2048,16]{2,0,1:T(8,128)(2,1)} copy(bf16[6,2048,16]{1,2,0:T(8,128)(2,1)S(1)} %maximum_bitcast_fusion) | data formatting | bytes 786432 | tf_op jit(solution)/shard_map/transpose | solution.py:177
  20.0 5.6 %reshape.550 = bf16[128,2,768]{2,1,0:T(2,128)(2,1)S(1)} reshape(bf16[2048,6,16]{2,1,0:T(8,128)(2,1)} %bitcast.270) | data formatting | bytes 786432
  25.6 23.8 %all_to_all.48 = bf16[128,2,768]{2,1,0:T(2,128)(2,1)S(1)} all-to-all(bf16[128,2,768]{2,1,0:T(2,128)(2,1)S(1)} %reshape.550), channel_id=1, replica_groups=mesh['wide'=16,'grp'=8] {'wide','grp'}, dimensions={0} | all-to-all | bytes 786432 | tf_op jit(solution)/shard_map/all_to_all | solution.py:180
  49.4 4.8 %reshape.551 = bf16[2048,6,16]{2,1,0:T(8,128)(2,1)} reshape(bf16[128,2,768]{2,1,0:T(2,128)(2,1)S(1)} %all_to_all.48) | data formatting | bytes 786432
  54.3 6.1 %copy.158 = bf16[6,128,16,16]{2,1,3,0:T(8,128)(2,1)S(1)} copy(bf16[6,128,16,16]{3,0,2,1:T(8,128)(2,1)} %bitcast.269) | data formatting | bytes 786432 | tf_op jit(solution)/shard_map/all_to_all | solution.py:180
  60.4 1.9 fusion.250
  62.3 4.3 %copy.126 = bf16[3,16,128,16]{3,2,1,0:T(8,128)(2,1)S(1)} copy(bf16[3,16,128,16]{1,2,3,0:T(8,128)(2,1)} %get-tuple-element.58) | data formatting | bytes 393216 | tf_op jit(solution)/shard_map/slice | solution.py:181
  67.4 1.2 fusion.99
  68.7 1.2 fusion.106
  69.9 3.1 copy.127
  73.8 1.5 convolution_add_fusion
  75.3 1.4 convolution_subtract_fusion.1
  77.6 3.4 copy.159
  81.0 1.9 reshape.552
  82.9 9.3 %all_to_all.49 = bf16[8,2,6144]{2,1,0:T(2,128)(2,1)S(1)} all-to-all(bf16[8,2,6144]{2,1,0:T(2,128)(2,1)S(1)} %reshape.552), channel_id=1, replica_groups=mesh['wide'=16,'grp'=8] {'grp'}, dimensions={0} | all-to-all | bytes 393216 | tf_op jit(solution)/shard_map/all_to_all | solution.py:182
  92.2 2.0 reshape.553
  94.2 2.0 copy.161
  100.3 1.0 copy.160
  101.5 38.9 %all-gather.2.cloned.1.call-done = bf16[3,2048,256]{2,1,0:T(8,128)(2,1)} async-done(((bf16[3,128,256]{2,1,0:T(8,128)(2,1)}), bf16[3,2048,256]{2,1,0:T(8,128)(2,1)}) %all-gather.2.cloned.1.call-update) | async-done | bytes 3145744 | tf_op jit(solution)/shard_map/all_gather | solution.py:206
  140.4 5.1 %convert_element_type.418 = f32[3,2048,256]{2,1,0:T(8,128)} convert(bf16[3,2048,256]{2,1,0:T(8,128)(2,1)} %all-gather.2.cloned.1.call-done) | non-fusion elementwise | flops 1572864 | bytes 9437184 | tf_op jit(solution)/shard_map/convert_element_type | solution.py:208
  145.4 5.9 %while.1 = (s32[]{:T(128)}, f32[3,2048,256]{2,1,0:T(8,128)}, s32[2,3]{1,0:T(2,128)S(1)}, f32[2,3,64,64]{3,2,1,0:T(8,128)S(1)}, s32[]{:T(128)}) while((s32[]{:T(128)}, f32[3,2048,256]{2,1,0:T(8,128)}, s32[2,3]{1,0:T(2,128)S(1)}, f32[2,3,64,64]{3,2,1,0:T(8,128)S(1)}, s32[]{:T(128)}) %tuple.62), condition=%wide.while_cond, body=%wide.while_body.sunk | while | flops 2 | bytes 147581 | solution.py:211
  146.1 2.3 bitcast_dynamic-update-slice_fusion.2
  149.0 2.3 bitcast_dynamic-update-slice_fusion.2
  153.2 3.9 %fusion.8 = f32[2,64,128,128]{3,2,1,0:T(8,128)S(1)} fusion(bf16[2,1,64,128,128]{4,3,2,1,0:T(8,128)(2,1)} %param.7, f32[128,128]{1,0:T(8,128)S(1)} %get-tuple-element.89, f32[64]{0:T(128)S(1)} %fusion.158, f32[2,128,128]{2,1,0:T(8,128)S(1)} %copy.134, f32[128,128]{1,0:T(8,128)S(1)} %get-tuple-element.88), kind=kLoop, calls=%fused_computation.23 | loop fusion | flops 16777216 | bytes 12845312 | tf_op jit(solution)/shard_map/vmap()/add | solution.py:85
  157.3 7.7 %fusion.247 = (f32[2,64,128,1]{3,2,1,0:T(8,128)}, f32[2,64,128,1]{3,2,1,0:T(8,128)}) fusion(f32[2,64,128,128]{3,2,1,0:T(8,128)S(1)} %fusion.8), kind=kLoop, calls=%fused_computation.372 | loop fusion | bytes 262144 | tf_op jit(solution)/shard_map/vmap(jit(_pad))/slice | solution.py:59
  166.1 5.4 %broadcast_multiply_fusion.1 = (f32[2,64,128,128]{3,2,1,0:T(8,128)}, f32[2,64,128,128]{3,2,1,0:T(8,128)S(1)}) fusion(f32[64]{0:T(128)S(1)} %multiply_exponential_fusion, f32[2,128,128]{2,1,0:T(8,128)S(1)} %copy.137, f32[2,128,128]{2,1,0:T(8,128)S(1)} %copy.139), kind=kLoop, calls=%fused_computation.26 | loop fusion | flops 4194304 | bytes 17039616 | tf_op jit(solution)/shard_map/vmap()/mul | solution.py:87
  171.5 3.2 copy-done.1
  174.9 13.3 %fusion.246 = (f32[2,64,128,1]{3,2,1,0:T(8,128)}, f32[2,64,128,1]{3,2,1,0:T(8,128)}) fusion(f32[2,64,128,128]{3,2,1,0:T(8,128)} %get-tuple-element.86), kind=kLoop, calls=%fused_computation.371 | loop fusion | bytes 262144 | tf_op jit(solution)/shard_map/vmap(jit(_pad))/slice | solution.py:60
  188.2 12.6 %fusion.3 = f32[2,64,129,128]{3,2,1,0:T(8,128)} fusion(f32[2,64,128,128]{3,2,1,0:T(8,128)S(1)} %bitcast.266, f32[2,64,1,128]{3,2,1,0:T(1,128)S(1)} %get-tuple-element.56, f32[2,64,1,128]{3,2,1,0:T(1,128)S(1)} %get-tuple-element.55, f32[2,64,1,128]{3,2,1,0:T(1,128)S(1)} %get-tuple-element.54, f32[2,64,128,128]{3,2,1,0:T(8,128)} %copy-done.1, ...), kind=kLoop, calls=%fused_computation.14 | loop fusion | flops 23248896 | bytes 25493504 | tf_op jit(solution)/shard_map/vmap()/add | solution.py:68
  200.8 25.9 %fusion.1 = f32[2,64,128,129]{3,2,1,0:T(8,128)} fusion(f32[2,64,128,128]{3,2,1,0:T(8,128)S(1)} %bitcast.266, f32[2,64,128,1]{3,2,1,0:T(8,128)} %get-tuple-element.52, f32[2,64,128,1]{3,2,1,0:T(8,128)} %get-tuple-element.51, f32[2,64,128,1]{3,2,1,0:T(8,128)} %get-tuple-element.50, f32[2,64,128,128]{3,2,1,0:T(8,128)} %get-tuple-element.86, ...), kind=kLoop, calls=%fused_computation.9 | loop fusion | flops 23248896 | bytes 25493504 | tf_op jit(solution)/shard_map/vmap()/add | solution.py:68
  226.7 22.0 %convert_bitcast_fusion = (bf16[2,1,64,128,128]{4,3,2,1,0:T(8,128)(2,1)}, f32[2,64,128,128]{3,2,1,0:T(8,128)}) fusion(f32[2,64,129,128]{3,2,1,0:T(8,128)} %fusion.3, f32[2,64,128,129]{3,2,1,0:T(8,128)} %fusion.1, bf16[2,1,64,128,128]{4,3,2,1,0:T(8,128)(2,1)} %param.7, f32[128,128]{1,0:T(8,128)S(1)} %get-tuple-element.89, f32[64]{0:T(128)S(1)} %fusion.158, ...), kind=kLoop, calls=%fused_computation.24 | loop fusion | flops 31457280 | bytes 50594048 | tf_op jit(solution)/shard_map/broadcast_in_dim | solution.py:251
  248.7 3.8 %reduce_sum.29 = f32[2,128,128]{2,1,0:T(8,128)S(1)} reduce(f32[2,64,128,128]{3,2,1,0:T(8,128)} %get-tuple-element.44, f32[]{:T(128)} %constant.206.clone.1), dimensions={1}, to_apply=%region_1.2 | reduce | flops 2064384 | bytes 8519684 | tf_op jit(solution)/shard_map/vmap()/reduce_sum | solution.py:93
  252.5 9.8 %add.542 = f32[2,64,2,64,2]{4,3,2,1,0:T(8,128)} reshape(f32[2,128,128]{2,1,0:T(8,128)S(1)} %multiply_add_fusion) | data formatting | bytes 262144 | tf_op jit(solution)/shard_map/vmap()/add | solution.py:93
  262.3 4.5 %reduce_sum.30 = f32[2,64,64]{2,1,0:T(8,128)S(1)} reduce(f32[2,64,2,64,2]{4,3,2,1,0:T(8,128)} %add.542, f32[]{:T(128)} %constant.206.clone.1), dimensions={2,4}, to_apply=%region_2.3 | reduce | flops 24576 | bytes 163844 | tf_op jit(solution)/shard_map/vmap()/reduce_sum | solution.py:94
  267.0 17.1 %all_gather.7 = bf16[2,16,4096]{2,0,1:T(2,128)(2,1)S(1)} all-gather(bf16[2,1,4096]{2,0,1:T(2,128)(2,1)S(1)} %convert_element_type.422), channel_id=1, replica_groups=mesh['wide'=16,'grp'=8] {'wide'}, dimensions={1}, use_global_device_ids=true | all-gather | bytes 278528 | tf_op jit(solution)/shard_map/all_gather | solution.py:221
  285.3 6.6 %collective-permute-start = (bf16[16,256]{1,0:T(8,128)(2,1)S(1)}, bf16[16,256]{1,0:T(8,128)(2,1)S(1)}, u32[]{:S(2)}, u32[]{:S(2)}) collective-permute-start(bf16[16,256]{1,0:T(8,128)(2,1)S(1)} %get-tuple-element.84), channel_id=1, source_target_pairs={{0,1},{1,0},{2,3},{3,2},{4,5},{5,4},{6,7},{7,6},{8,9},{9,8},{10,11... | collective-permute-start | bytes 24584 | tf_op jit(solution)/shard_map/ppermute | solution.py:37
  292.4 2.3 collective-permute-start.6
  295.0 2.1 collective-permute-start.4
  297.1 1.5 collective-permute-start.3
  298.7 2.8 collective-permute-done.1
  301.5 1.3 collective-permute-start.2
  302.7 2.0 collective-permute-done.2
  309.1 1.5 reshape.554
  310.7 6.5 %all-to-all-start.2 = ((bf16[128,2,256]{2,1,0:T(2,128)(2,1)}), bf16[128,2,256]{2,1,0:T(2,128)(2,1)S(1)}, u32[]{:S(2)}, u32[]{:S(2)}) async-start(bf16[128,2,256]{2,1,0:T(2,128)(2,1)} %reshape.554), calls=%async_computation.2 | async-start | bytes 262144 | tf_op jit(solution)/shard_map/all_to_all | solution.py:248
  317.8 9.3 %all-to-all-done.2 = bf16[128,2,256]{2,1,0:T(2,128)(2,1)S(1)} async-done(((bf16[128,2,256]{2,1,0:T(2,128)(2,1)}), bf16[128,2,256]{2,1,0:T(2,128)(2,1)S(1)}, u32[]{:S(2)}, u32[]{:S(2)}) %all-to-all-start.2) | async-done | bytes 131104 | tf_op jit(solution)/shard_map/all_to_all | solution.py:248
  327.8 2.0 copy.162
  329.9 1.1 copy.150
  331.8 1.1 copy.151
  (165 shorter events, 31.5 us)
Async XLA Ops:
  7.2 133.2 %all-gather.2.cloned.1.call-start = ((), (), s32[]{:S(2)}) async-start(), calls=%async_computation.3 | async-start | bytes 3342336 | tf_op jit(solution)/shard_map/all_gather | solution.py:206
  7.3 6.4 %copy-start.3 = (f32[32,64]{1,0:T(8,128)}, f32[32,64]{1,0:T(8,128)S(1)}, u32[]{:S(2)}) copy-start(f32[32,64]{1,0:T(8,128)S(1)} %get-tuple-element.98) | copy-start | bytes 24580
  62.3 7.6 %copy-start.2 = (bf16[3,16,128,16]{1,2,3,0:T(8,128)(2,1)S(1)}, bf16[3,16,128,16]{1,2,3,0:T(8,128)(2,1)}, u32[]{:S(2)}) copy-start(bf16[3,16,128,16]{1,2,3,0:T(8,128)(2,1)} %get-tuple-element.57) | copy-start | bytes 589828
  69.9 6.8 %copy-start.4 = (f32[32,64]{1,0:T(8,128)S(1)}, f32[32,64]{1,0:T(8,128)}, u32[]{:S(2)}) copy-start(f32[32,64]{1,0:T(8,128)} %copy-done.3) | copy-start | bytes 24580
  76.7 19.6 %copy-start.8 = (s32[256]{0:T(256)S(1)}, s32[256]{0:T(256)}, u32[]{:S(2)}) copy-start(s32[256]{0:T(256)} %param.6) | copy-start | bytes 3076
  151.3 0.7 copy-start.5
  157.2 8.4 %copy-start = (f32[2,64,128,128]{3,2,1,0:T(8,128)}, f32[2,64,128,128]{3,2,1,0:T(8,128)S(1)}, u32[]{:S(2)}) copy-start(f32[2,64,128,128]{3,2,1,0:T(8,128)S(1)} %fusion.8) | copy-start | bytes 25165828
  166.1 22.1 %slice-start = ((s8[8388608]{0:T(1024)(128)(4,1)}), s8[4194304]{0:T(1024)(128)(4,1)S(1)}, s32[]{:S(2)}) async-start(s8[8388608]{0:T(1024)(128)(4,1)} %bitcast.265), calls=%async_computation.4 | async-start | bytes 8388608
  171.5 3.2 copy-start.1
  174.9 13.3 %slice-start.1 = ((s8[8388608]{0:T(1024)(128)(4,1)}), s8[4194304]{0:T(1024)(128)(4,1)S(1)}, s32[]{:S(2)}) async-start(s8[8388608]{0:T(1024)(128)(4,1)} %bitcast.265), calls=%async_computation.5 | async-start | bytes 8388608
  252.5 32.5 %copy-start.7 = (pred[2,4]{1,0:T(4,128)(4,1)S(1)}, pred[2,4]{1,0:T(4,128)(4,1)}, u32[]{:S(2)}) copy-start(pred[2,4]{1,0:T(4,128)(4,1)} %broadcast_in_dim.29) | copy-start | bytes 28
  262.3 43.6 %copy-start.6 = (f32[32,64]{1,0:T(8,128)S(1)}, f32[32,64]{1,0:T(8,128)}, u32[]{:S(2)}) copy-start(f32[32,64]{1,0:T(8,128)} %get-tuple-element.101) | copy-start | bytes 24580
  285.3 13.3 %collective-permute-start = (bf16[16,256]{1,0:T(8,128)(2,1)S(1)}, bf16[16,256]{1,0:T(8,128)(2,1)S(1)}, u32[]{:S(2)}, u32[]{:S(2)}) collective-permute-start(bf16[16,256]{1,0:T(8,128)(2,1)S(1)} %get-tuple-element.84), channel_id=1, source_target_pairs={{0,1},{1,0},{2,3},{3,2},{4,5},{5,4},{6,7},{7,6},{8,9},{9,8},{10,11... | collective-permute-start | bytes 24584 | tf_op jit(solution)/shard_map/ppermute | solution.py:37
  292.4 12.4 %collective-permute-start.6 = (bf16[16,256]{1,0:T(8,128)(2,1)S(1)}, bf16[16,256]{1,0:T(8,128)(2,1)S(1)}, u32[]{:S(2)}, u32[]{:S(2)}) collective-permute-start(bf16[16,256]{1,0:T(8,128)(2,1)S(1)} %get-tuple-element.78), channel_id=1, source_target_pairs={{0,7},{1,6},{2,5},{3,4},{4,3},{5,2},{6,1},{7,0},{8,15},{9,14},{10,... | collective-permute-start | bytes 24584 | tf_op jit(solution)/shard_map/ppermute | solution.py:37
  294.7 10.0 %collective-permute-start.5 = (bf16[16,256]{1,0:T(8,128)(2,1)S(1)}, bf16[16,256]{1,0:T(8,128)(2,1)S(1)}, u32[]{:S(2)}, u32[]{:S(2)}) collective-permute-start(bf16[16,256]{1,0:T(8,128)(2,1)S(1)} %get-tuple-element.79), channel_id=1, source_target_pairs={{0,6},{1,7},{2,4},{3,5},{4,2},{5,3},{6,0},{7,1},{8,14},{9,15},{10,... | collective-permute-start | bytes 24584 | tf_op jit(solution)/shard_map/ppermute | solution.py:37
  295.0 9.7 %collective-permute-start.4 = (bf16[16,256]{1,0:T(8,128)(2,1)S(1)}, bf16[16,256]{1,0:T(8,128)(2,1)S(1)}, u32[]{:S(2)}, u32[]{:S(2)}) collective-permute-start(bf16[16,256]{1,0:T(8,128)(2,1)S(1)} %get-tuple-element.80), channel_id=1, source_target_pairs={{0,5},{1,4},{2,7},{3,6},{4,1},{5,0},{6,3},{7,2},{8,13},{9,12},{10,... | collective-permute-start | bytes 24584 | tf_op jit(solution)/shard_map/ppermute | solution.py:37
  297.1 7.6 %collective-permute-start.3 = (bf16[16,256]{1,0:T(8,128)(2,1)S(1)}, bf16[16,256]{1,0:T(8,128)(2,1)S(1)}, u32[]{:S(2)}, u32[]{:S(2)}) collective-permute-start(bf16[16,256]{1,0:T(8,128)(2,1)S(1)} %get-tuple-element.81), channel_id=1, source_target_pairs={{0,4},{1,5},{2,6},{3,7},{4,0},{5,1},{6,2},{7,3},{8,12},{9,13},{10,... | collective-permute-start | bytes 24584 | tf_op jit(solution)/shard_map/ppermute | solution.py:37
  298.7 2.8 collective-permute-start.1
  301.5 3.2 collective-permute-start.2
  310.7 16.4 %all-to-all-start.2 = ((bf16[128,2,256]{2,1,0:T(2,128)(2,1)}), bf16[128,2,256]{2,1,0:T(2,128)(2,1)S(1)}, u32[]{:S(2)}, u32[]{:S(2)}) async-start(bf16[128,2,256]{2,1,0:T(2,128)(2,1)} %reshape.554), calls=%async_computation.2 | async-start | bytes 262144 | tf_op jit(solution)/shard_map/all_to_all | solution.py:248
Sparse Core Ops, SparseCore 0:
  96.4 43.9 all-gather.1
